TPU v7x, 32 devices: a whole 2x2x4 slice. The times are simulated.
32 devices in a mesh: seq: 8 (over z, core), blk: 4 (over y, x).
Axes of the slice: x: 2, y: 2, z: 4, core: 2. Of those that a mesh axis runs over, the one named last changes fastest.
Arguments:
- tokens: bfloat16 [8192, 8192], P('seq', 'blk'), may hold values from -6 to 6
- right_factor: bfloat16 [64, 128, 128], P('blk', 'seq'), may hold values from -0.5 to 0.5
- left_factor: bfloat16 [128, 64, 64], P('blk', 'seq'), may hold values from -0.75 to 0.75
- target: bfloat16 [8192, 8192], P('seq', 'blk'), may hold values from -4 to 4
Outputs:
- student: bfloat16 [8192, 8192], P('seq', 'blk')
- right_grad: float32 [64, 128, 128], P('blk', 'seq')
- left_grad: float32 [128, 64, 64], P('blk', 'seq')
All inputs are finite; a program needn't handle non-finite values.
Results may differ from a plain program's by a relative error of at most 0.017.
Values may be sent and summed in bfloat16 or wider, within the bound.
A program may use at most 64 MiB of HBM per device.

v0:
```python
import jax
import jax.numpy as jnp
from jax import lax
from jax.sharding import PartitionSpec as P


def gelu_tanh(values):
    return jax.nn.gelu(values, approximate=True)


def shards(tokens, right_factor, left_factor, target):
    rows = tokens.shape[0]
    count = rows * lax.axis_size("seq")
    scale = 1.0 / jnp.sqrt(jnp.float32(count))
    right_full, left_full = (
        lax.all_gather(right_factor, "seq", axis=1, tiled=True),
        lax.all_gather(left_factor, "seq", axis=1, tiled=True),
    )
    nblocks = left_full.shape[1]
    local_blocks = right_full.shape[0]
    width = right_full.shape[1]
    inputs = tokens.reshape(rows, local_blocks, width)
    mixed = jnp.einsum(
        "tki,kci->tkc", inputs, right_full, preferred_element_type=jnp.float32
    ).astype(jnp.bfloat16)
    turned = lax.all_to_all(mixed, "blk", split_axis=2, concat_axis=1, tiled=True)
    turned, pre = (
        turned,
        jnp.einsum("tkc,cmk->tcm", turned, left_full, preferred_element_type=jnp.float32),
    )
    local_cols = pre.shape[1]
    act, back = jax.vjp(gelu_tanh, pre)
    student = act.reshape(rows, local_cols * nblocks).astype(jnp.bfloat16)
    residual = (act - target.reshape(rows, local_cols, nblocks).astype(jnp.float32)) * scale
    pre_grad = back(residual)[0].astype(jnp.bfloat16)
    turned_grad = jnp.einsum(
        "tcm,cmk->tkc", pre_grad, left_full, preferred_element_type=jnp.float32
    ).astype(jnp.bfloat16)
    mixed_grad = lax.all_to_all(turned_grad, "blk", split_axis=1, concat_axis=2, tiled=True)
    left_term = jnp.einsum("tcm,tkc->cmk", pre_grad, turned, preferred_element_type=jnp.float32)
    right_term = jnp.einsum("tkc,tki->kci", mixed_grad, inputs, preferred_element_type=jnp.float32)
    right_total, left_total = (
        lax.psum(right_term.astype(jnp.bfloat16), "seq").astype(jnp.float32),
        lax.psum(left_term.astype(jnp.bfloat16), "seq").astype(jnp.float32),
    )
    place = lax.axis_index("seq")
    right_rows = right_factor.shape[1]
    left_rows = left_factor.shape[1]
    right_grad = lax.dynamic_slice_in_dim(right_total, place * right_rows, right_rows, 1)
    left_grad = lax.dynamic_slice_in_dim(left_total, place * left_rows, left_rows, 1)
    return (student, right_grad, left_grad)


def solution(mesh):
    return jax.shard_map(
        shards,
        mesh=mesh,
        in_specs=(P("seq", "blk"), P("blk", "seq", None), P("blk", "seq", None), P("seq", "blk")),
        out_specs=(P("seq", "blk"), P("blk", "seq", None), P("blk", "seq", None)),
        check_vma=False,
    )
```

profile of v0, /device:TPU:0, one launch (start us, length us, event | category | flops | bytes accessed | tf_op | source)
XLA Modules:
  0.0 232.8 jit_solution(11892994726499473128)
XLA Ops:
  7.2 16.8 %all_gather.6 = bf16[16,128,128]{2,1,0:T(8,128)(2,1)S(1)} all-gather(bf16[16,16,128]{2,1,0:T(8,128)(2,1)} %param.5), channel_id=1, replica_groups=mesh['seq'=8,'blk'=4] {'seq'}, dimensions={1}, use_global_device_ids=true | all-gather | bytes 589824 | tf_op jit(solution)/shard_map/all_gather | solution.py:16
  24.0 3.5 %convert_bitcast_fusion.1 = bf16[1024,16,128]{0,2,1:T(8,128)(2,1)S(1)} fusion(bf16[16,128,128]{2,1,0:T(8,128)(2,1)S(1)} %all_gather.6, bf16[1024,2048]{1,0:T(8,128)(2,1)} %param.4), kind=kOutput, calls=%fused_computation.19 | convolution fusion | flops 538968064 | bytes 8912896 | tf_op jit(solution)/shard_map/tki,kci->tkc/dot_general | solution.py:23
  27.4 4.3 %copy.14 = bf16[1024,16,128]{0,1,2:T(8,128)(2,1)} copy(bf16[1024,16,128]{0,2,1:T(8,128)(2,1)S(1)} %convert_bitcast_fusion.1) | data formatting | bytes 8388608 | tf_op jit(solution)/shard_map/convert_element_type | solution.py:25
  31.8 4.9 %all-to-all-start = ((bf16[1024,16,128]{0,1,2:T(8,128)(2,1)}), bf16[1024,16,128]{0,1,2:T(8,128)(2,1)}, u32[]{:S(2)}, u32[]{:S(2)}) async-start(bf16[1024,16,128]{0,1,2:T(8,128)(2,1)} %copy.14), calls=%async_computation | async-start | bytes 8388608 | tf_op jit(solution)/shard_map/all_to_all | solution.py:26
  36.7 7.0 %copy.16 = f32[1024,2048]{0,1:T(8,128)} copy(bf16[1024,2048]{1,0:T(8,128)(2,1)} %param.7) | data formatting | bytes 12582912 | tf_op jit(solution)/shard_map/convert_element_type | solution.py:34
  43.7 13.7 %all_gather.7 = bf16[32,64,64]{2,1,0:T(8,128)(2,1)S(1)} all-gather(bf16[32,8,64]{2,1,0:T(8,128)(2,1)S(1)} %copy-done.4), channel_id=1, replica_groups=mesh['seq'=8,'blk'=4] {'seq'}, dimensions={1}, use_global_device_ids=true | all-gather | bytes 294912 | tf_op jit(solution)/shard_map/all_gather | solution.py:17
  57.4 27.5 %all-to-all-done = bf16[1024,16,128]{0,1,2:T(8,128)(2,1)} async-done(((bf16[1024,16,128]{0,1,2:T(8,128)(2,1)}), bf16[1024,16,128]{0,1,2:T(8,128)(2,1)}, u32[]{:S(2)}, u32[]{:S(2)}) %all-to-all-start) | async-done | bytes 4194336 | tf_op jit(solution)/shard_map/all_to_all | solution.py:26
  84.9 2.8 %copy.15 = bf16[1024,16,4,32]{0,1,2,3:T(8,128)(2,1)S(1)} copy(bf16[1024,16,4,32]{0,1,3,2:T(8,128)(2,1)} %bitcast.1) | data formatting | bytes 8388608 | tf_op jit(solution)/shard_map/all_to_all | solution.py:26
  87.7 3.3 %copy-done.2 = f32[1024,2048]{0,1:T(8,128)S(1)} copy-done((f32[1024,2048]{0,1:T(8,128)S(1)}, f32[1024,2048]{0,1:T(8,128)}, u32[]{:S(2)}) %copy-start.2) | copy-done | bytes 8388632
  91.1 8.5 %fusion.6 = (bf16[1024,32,64]{0,2,1:T(8,128)(2,1)S(1)}, bf16[1024,32,64]{0,2,1:T(8,128)(2,1)}) fusion(f32[1024,32,64]{0,2,1:T(8,128)S(1)} %bitcast.59, bf16[32,64,64]{2,1,0:T(8,128)(2,1)S(1)} %all_gather.7, bf16[1024,64,32]{0,1,2:T(8,128)(2,1)S(1)} %bitcast.57), kind=kOutput, calls=%fused_computation.8 | convolution fusion | flops 318767104 | bytes 21233664 | tf_op jit(solution)/shard_map/tkc,cmk->tcm/dot_general | solution.py:29
  99.5 1.3 convert_bitcast_fusion
  100.8 0.6 copy-done.1
  101.4 4.3 %copy.17 = bf16[1024,64,32]{0,2,1:T(8,128)(2,1)} copy(bf16[1024,64,32]{0,1,2:T(8,128)(2,1)S(1)} %convert_bitcast_fusion) | data formatting | bytes 8388608 | tf_op jit(solution)/shard_map/convert_element_type | solution.py:38
  105.8 4.8 %all-to-all-start.1 = ((bf16[1024,64,32]{0,2,1:T(8,128)(2,1)}), bf16[1024,64,32]{0,2,1:T(8,128)(2,1)}, u32[]{:S(2)}, u32[]{:S(2)}) async-start(bf16[1024,64,32]{0,2,1:T(8,128)(2,1)} %copy.17), calls=%async_computation.1 | async-start | bytes 8388608 | tf_op jit(solution)/shard_map/all_to_all | solution.py:39
  110.6 0.2 all-reduce.3.cloned.1.call-start
  110.9 5.5 %convolution_convert_fusion = bf16[32,64,64]{2,1,0:T(8,128)(2,1)} fusion(bf16[1024,32,64]{0,2,1:T(8,128)(2,1)} %copy-done.1, bf16[1024,64,32]{0,1,2:T(8,128)(2,1)} %bitcast.58), kind=kOutput, calls=%fused_computation.23 | convolution fusion | flops 268566528 | bytes 8650752 | tf_op jit(solution)/shard_map/tcm,tkc->cmk/dot_general | solution.py:40
  116.4 41.6 %all-to-all-done.1 = bf16[1024,64,32]{0,2,1:T(8,128)(2,1)} async-done(((bf16[1024,64,32]{0,2,1:T(8,128)(2,1)}), bf16[1024,64,32]{0,2,1:T(8,128)(2,1)}, u32[]{:S(2)}, u32[]{:S(2)}) %all-to-all-start.1) | async-done | bytes 4194336 | tf_op jit(solution)/shard_map/all_to_all | solution.py:39
  158.0 2.8 %copy.18 = bf16[1024,4,16,32]{0,3,1,2:T(8,128)(2,1)S(1)} copy(bf16[1024,4,16,32]{0,3,2,1:T(8,128)(2,1)} %bitcast.8) | data formatting | bytes 8388608 | tf_op jit(solution)/shard_map/all_to_all | solution.py:39
  160.8 0.6 copy-done.3
  161.5 2.3 fusion.18
  163.8 6.4 %copy.20 = bf16[1024,2048]{1,0:T(8,128)(2,1)} copy(bf16[1024,2048]{0,1:T(8,128)(2,1)} %bitcast.60) | data formatting | bytes 8388608
  170.2 52.7 %all-reduce.3.cloned.1.call-done = (bf16[16,128,128]{2,1,0:T(8,128)(2,1)}, bf16[32,64,64]{2,1,0:T(8,128)(2,1)}) async-done(((bf16[16,128,128]{2,1,0:T(8,128)(2,1)}, bf16[32,64,64]{2,1,0:T(8,128)(2,1)}), (bf16[16,128,128]{2,1,0:T(8,128)(2,1)}, bf16[32,64,64]{2,1,0:T(8,128)(2,1)})) %all-reduce.3.cloned.1.call-update) | async-done | bytes 786448 | tf_op jit(solution)/shard_map/psum | solution.py:43
  223.0 1.5 dynamic-slice_convert_fusion
  224.5 1.5 dynamic-slice_convert_fusion.1
  (8 shorter events, 0.0 us)
Async XLA Ops:
  31.8 53.1 %all-to-all-start = ((bf16[1024,16,128]{0,1,2:T(8,128)(2,1)}), bf16[1024,16,128]{0,1,2:T(8,128)(2,1)}, u32[]{:S(2)}, u32[]{:S(2)}) async-start(bf16[1024,16,128]{0,1,2:T(8,128)(2,1)} %copy.14), calls=%async_computation | async-start | bytes 8388608 | tf_op jit(solution)/shard_map/all_to_all | solution.py:26
  36.7 7.0 %copy-start.4 = (bf16[32,8,64]{2,1,0:T(8,128)(2,1)S(1)}, bf16[32,8,64]{2,1,0:T(8,128)(2,1)}, u32[]{:S(2)}) copy-start(bf16[32,8,64]{2,1,0:T(8,128)(2,1)} %param.6) | copy-start | bytes 98308
  84.9 6.2 %copy-start.2 = (f32[1024,2048]{0,1:T(8,128)S(1)}, f32[1024,2048]{0,1:T(8,128)}, u32[]{:S(2)}) copy-start(f32[1024,2048]{0,1:T(8,128)} %copy.16) | copy-start | bytes 25165828
  87.7 11.8 %copy-start = (bf16[1024,16,4,32]{0,1,2,3:T(8,128)(2,1)}, bf16[1024,16,4,32]{0,1,2,3:T(8,128)(2,1)S(1)}, u32[]{:S(2)}) copy-start(bf16[1024,16,4,32]{0,1,2,3:T(8,128)(2,1)S(1)} %copy.15) | copy-start | bytes 12582916
  99.5 1.9 copy-start.1
  105.8 52.2 %all-to-all-start.1 = ((bf16[1024,64,32]{0,2,1:T(8,128)(2,1)}), bf16[1024,64,32]{0,2,1:T(8,128)(2,1)}, u32[]{:S(2)}, u32[]{:S(2)}) async-start(bf16[1024,64,32]{0,2,1:T(8,128)(2,1)} %copy.17), calls=%async_computation.1 | async-start | bytes 8388608 | tf_op jit(solution)/shard_map/all_to_all | solution.py:39
  110.6 112.3 %all-reduce.3.cloned.1.call-start = ((), (), s32[]{:S(2)}) async-start(), calls=%async_computation.2 | async-start | bytes 2097152 | tf_op jit(solution)/shard_map/psum | solution.py:43
  158.0 3.4 %copy-start.3 = (bf16[1024,2048]{1,0:T(8,128)(2,1)S(1)}, bf16[1024,2048]{1,0:T(8,128)(2,1)}, u32[]{:S(2)}) copy-start(bf16[1024,2048]{1,0:T(8,128)(2,1)} %param.4) | copy-start | bytes 12582916
Sparse Core Ops, SparseCore 0:
  163.9 59.0 all-reduce.2
where the time goes:
time: 233 us
  waiting for transfers between devices  122 us (52%)
  local copies, waits for them, and re-layouts  32.3 us (14%)
  blocking collectives  30.5 us (13%)
  matrix products  21 us (9%)
  between operations  14.1 us (6%)
  starting transfers between devices  9.98 us (4%)
  other arithmetic  3.01 us (1%)
    psum x1, waiting for transfers between devices, shards(): lax.psum(right_term.astype(jnp.bfloat16), 'seq').astype(jnp.float32)  52.7 us
    all_to_all x1, waiting for transfers between devices, shards(): lax.all_to_all(turned_grad, 'blk', split_axis=1, concat_axis=2, tiled=True)  41.6 us
    all_to_all x1, waiting for transfers between devices, shards(): lax.all_to_all(mixed, 'blk', split_axis=2, concat_axis=1, tiled=True)  27.5 us
    all_gather x1, blocking collectives, shards(): lax.all_gather(right_factor, 'seq', axis=1, tiled=True)  16.8 us
    all_gather x1, blocking collectives, shards(): lax.all_gather(left_factor, 'seq', axis=1, tiled=True)  13.7 us
    unnamed x11, local copies, waits for them, and re-layouts  11 us
    dot_general x1, matrix products, shards(): jnp.einsum('tkc,cmk->tcm', turned, left_full, preferred_element_type=jnp....  8.46 us
    convert_element_type x1, local copies, waits for them, and re-layouts, shards(): target.reshape(rows, local_cols, nblocks).astype(jnp.float32)  6.96 us
  transfers between devices with their start and end apart: 3, of which 3 were waited for; matrix products, arithmetic and copies ran while one was open for 8% of the time, Pallas kernels for 0%

commit v1 on v0

v1 whole, which is shorter than its diff:
```python
import functools
import math

import jax
import jax.numpy as jnp
from jax import lax
from jax.experimental import pallas as pl
from jax.experimental.pallas import tpu as pltpu
from jax.sharding import PartitionSpec as P

MESH = pl.DeviceIdType.MESH
F32 = jnp.float32
BF16 = jnp.bfloat16
C0 = math.sqrt(2.0 / math.pi)
NT = (((1,), (1,)), ((), ()))
NN = (((1,), (0,)), ((), ()))


def dot(a, b, dims):
    return lax.dot_general(a, b, dims, preferred_element_type=F32)


def partner(b, d, size):
    step, out = 1, b
    while step < size:
        if (d // step) % 2:
            out = out + step * (1 - 2 * ((b // step) % 2))
        step *= 2
    return out


def stack(parts):
    if parts[0].shape[0] % 16:
        return jnp.concatenate([v.astype(F32) for v in parts], axis=0).astype(BF16)
    return jnp.concatenate(parts, axis=0)


def eye(n):
    return (
        lax.broadcasted_iota(jnp.int32, (n, n), 0) == lax.broadcasted_iota(jnp.int32, (n, n), 1)
    ).astype(F32).astype(BF16)


def kernel(
    cfg, x_hbm, f_hbm, t_hbm, st_hbm, rg_out, lg_out,
    xv, tv, stv, snd, recv, bsnd, brecv, fm, ft,
    gat, gf, rfull, lc, wb, wt, rg, lg, lga, idt,
    pbr, sibr, zsr, zrr, pbl, sibl, zsl, zrl,
    sx, sto, sf, gs, gr, fs, fr,
    as_, ar, al, bs, br, bl,
    rs1, rr1, rs2, rr2, ls1, lr1, ls2, lr2,
):
    S, B, NC, tc, kl, cl, nb, w, r, lr = cfg
    Q = S // 2
    H = tc // 128
    s = lax.axis_index("seq")
    b = lax.axis_index("blk")
    q, core = s // 2, s % 2
    scale = 1.0 / math.sqrt(float(S * NC * tc))
    rrows, lrows = kl * r, (cl // 2) * lr
    sib = (s + 1 - 2 * core, b)
    zpeers = [((((q + o) % Q) * 2 + core), b) for o in range(1, Q)]
    bids = [partner(b, d, B) for d in range(B - 1, 0, -1)]
    bpeers = [(s, i) for i in bids]

    def xload(j):
        return pltpu.make_async_copy(x_hbm.at[pl.ds(pl.multiple_of(j * tc, tc), tc)], xv.at[j], sx.at[0, j])

    def tload(j):
        return pltpu.make_async_copy(t_hbm.at[pl.ds(pl.multiple_of(j * tc, tc), tc)], tv.at[j], sx.at[1, j])

    def stout(j):
        return pltpu.make_async_copy(stv.at[j], st_hbm.at[pl.ds(pl.multiple_of(j * tc, tc), tc)], sto.at[j])

    own = pltpu.make_async_copy(f_hbm, gat.at[s], sf)
    own.start()
    for j in range(NC):
        xload(j).start()
    for j in range(NC):
        tload(j).start()

    barrier = pltpu.get_barrier_semaphore()
    for peer in [sib] + zpeers + bpeers:
        pl.semaphore_signal(barrier, inc=1, device_id=peer, device_id_type=MESH)
    pl.semaphore_wait(barrier, 1 + len(zpeers) + len(bpeers))

    own.wait()
    gsend = [
        pltpu.make_async_remote_copy(
            gat.at[s], gat.at[s], gs.at[o], gr.at[o], device_id=zpeers[o], device_id_type=MESH)
        for o in range(Q - 1)
    ]
    for c in gsend:
        c.start()

    def fwd_copy(o):
        src = ((q - o + Q) % Q) * 2 + core
        return pltpu.make_async_remote_copy(
            gat.at[src], gat.at[src], fs.at[o], fr.at[o], device_id=sib, device_id_type=MESH)

    fsend = [fwd_copy(o) for o in range(Q)]
    fsend[0].start()
    idt[...] = eye(tc)
    rg[...] = jnp.zeros_like(rg)
    lg[...] = jnp.zeros_like(lg)
    for o in range(1, Q):
        gsend[o - 1].wait_recv()
        fsend[o].start()
    for o in range(Q):
        fsend[o].wait_recv()

    for i in range(S):
        gf[i] = gat[i, :rrows, :].astype(F32).reshape(kl, r, w)

    def rbuild(k, _):
        rfull[k] = jnp.concatenate([gf[i, k] for i in range(S)], axis=0).astype(BF16)
        return 0

    lax.fori_loop(0, kl, rbuild, 0)

    def a_copy(j, d):
        return pltpu.make_async_remote_copy(
            snd.at[j, pl.ds(pl.multiple_of(bids[d] * cl, cl), cl)], recv.at[j, b],
            as_.at[j, d], ar.at[j, d], device_id=bpeers[d], device_id_type=MESH)

    def a_local(j):
        return pltpu.make_async_copy(
            snd.at[j, pl.ds(pl.multiple_of(b * cl, cl), cl)], recv.at[j, b], al.at[j])

    def forward(j, _):
        xload(j).wait()

        def mm(k, _):
            res = dot(rfull[k], xv[j, :, pl.ds(pl.multiple_of(k * w, w), w)], NT)
            for h in range(H):
                fm[h, pl.ds(pl.multiple_of(k * w, w), w), :] = res[:, h * 128:(h + 1) * 128]
            return 0

        lax.fori_loop(0, kl, mm, 0)

        def turn(g, _):
            for u in range(8):
                c = g * 8 + u
                for h in range(H):
                    snd[j, c, :, h * 128:(h + 1) * 128] = fm[h, pl.ds(c, kl, stride=w), :].astype(BF16)
            return 0

        lax.fori_loop(0, w // 8, turn, 0)
        for d in range(B - 1):
            a_copy(j, d).start()
        a_local(j).start()
        return 0

    lax.fori_loop(0, NC, forward, 0)

    gl = fm.at[0]
    lcols = lax.broadcasted_iota(jnp.int32, (nb, 128), 1)
    for i in range(S):
        gl[i * lrows:(i + 1) * lrows, :] = gat[i, rrows:rrows + lrows, :].astype(F32)
    e128 = eye(128)

    def lbuild(p, _):
        for m in range(lr):
            lc[pl.ds(m, S, stride=lr), :] = gl[pl.ds(p * lr + m, S, stride=lrows), :]
        v = lc[...]
        both = jnp.concatenate(
            [jnp.where(lcols < nb, v, 0.0), jnp.where(lcols >= nb, v, 0.0)], axis=0).astype(BF16)
        wb[p] = both
        wt[p] = dot(e128, both, NT).astype(BF16)
        return 0

    lax.fori_loop(0, cl // 2, lbuild, 0)

    def b_copy(j, d):
        return pltpu.make_async_remote_copy(
            bsnd.at[j, pl.ds(pl.multiple_of(bids[d] * kl, kl), kl)], brecv.at[j, b],
            bs.at[j, d], br.at[j, d], device_id=bpeers[d], device_id_type=MESH)

    def b_local(j):
        return pltpu.make_async_copy(
            bsnd.at[j, pl.ds(pl.multiple_of(b * kl, kl), kl)], brecv.at[j, b], bl.at[j])

    def middle(j, _):
        tload(j).wait()
        a_local(j).wait()
        for d in range(B - 1):
            a_copy(j, d).wait_recv()

        def pair(p, _):
            tp = stack([recv[j, a, 2 * p + c] for c in range(2) for a in range(B)])
            cols = pl.ds(pl.multiple_of(p * 128, 128), 128)
            v = dot(wb[p], tp, NN)
            tgt = dot(idt[:128, :128], tv[j, :, cols], NT)
            v2 = v * v
            th = jnp.tanh(v * (C0 + (C0 * 0.044715) * v2))
            half = 0.5 + 0.5 * th
            act = v * half
            deriv = half + 0.5 * v * (1.0 - th * th) * (C0 + (3.0 * 0.044715 * C0) * v2)
            pg = (((act - tgt) * scale) * deriv).astype(BF16)
            stv[j, :, cols] = dot(idt[...], act.astype(BF16), NT).astype(BF16)
            tg = dot(wt[p], pg, NN)
            for h in range(H):
                ft[h, pl.ds(pl.multiple_of(p * 128, 128), 128), :] = tg[:, h * 128:(h + 1) * 128]
            full = dot(pg, tp, NT)
            rows = pl.ds(pl.multiple_of(p * nb, nb), nb)
            lg[rows, :] += jnp.where(lcols < nb, full[:nb], full[nb:])
            return 0

        lax.fori_loop(0, cl // 2, pair, 0)

        def turn(g, _):
            for u in range(4):
                k = g * 4 + u
                for h in range(H):
                    bsnd[j, k, :, h * 128:(h + 1) * 128] = ft[h, pl.ds(k, cl, stride=nb), :].astype(BF16)
            return 0

        lax.fori_loop(0, nb // 4, turn, 0)
        for d in range(B - 1):
            b_copy(j, d).start()
        b_local(j).start()
        stout(j).start()
        return 0

    lax.fori_loop(0, NC, middle, 0)

    l1 = pltpu.make_async_remote_copy(
        pbl.at[1 - core], sibl, ls1, lr1, device_id=sib, device_id_type=MESH)
    for i in range(S):
        for m in range(lr):
            lga[pl.ds(m, cl // 2, stride=lr), :] = lg[pl.ds(i * lr + m, cl // 2, stride=nb), :]
        pbl[i % 2, i // 2] = lga[...].astype(BF16)
    l1.start()

    def right(j, _):
        b_local(j).wait()
        for d in range(B - 1):
            b_copy(j, d).wait_recv()

        def one(k, _):
            mg = stack([brecv[j, a, k] for a in range(B)])
            rg[k] += dot(mg, xv[j, :, pl.ds(pl.multiple_of(k * w, w), w)], NN)
            return 0

        lax.fori_loop(0, kl, one, 0)
        return 0

    def second(pb, sibv, zs, zr, ss, rs):
        for i in range(Q):
            zs[i] = (pb[core, i].astype(F32) + sibv[i].astype(F32)).astype(BF16)
        zr[q] = zs[q]
        copies = [
            pltpu.make_async_remote_copy(
                zs.at[(q + o + 1) % Q], zr.at[q], ss.at[o], rs.at[o],
                device_id=zpeers[o], device_id_type=MESH)
            for o in range(Q - 1)
        ]
        for c in copies:
            c.start()
        return copies

    def total(zr):
        acc = zr[0].astype(F32)
        for i in range(1, Q):
            acc = acc + zr[i].astype(F32)
        return acc

    right(0, 0)
    l1.wait_recv()
    l2 = second(pbl, sibl, zsl, zrl, ls2, lr2)
    lax.fori_loop(1, NC, right, 0)

    for i in range(S):
        pbr[i % 2, i // 2] = rg[:, i * r:(i + 1) * r, :].reshape(rrows, w).astype(BF16)
    r1 = pltpu.make_async_remote_copy(
        pbr.at[1 - core], sibr, rs1, rr1, device_id=sib, device_id_type=MESH)
    r1.start()
    for c in l2:
        c.wait_recv()
    lg_out[...] = total(zrl)
    r1.wait_recv()
    r2 = second(pbr, sibr, zsr, zrr, rs2, rr2)
    for c in gsend + fsend + [l1, r1] + l2:
        c.wait_send()

    def drain(j, _):
        for d in range(B - 1):
            a_copy(j, d).wait_send()
            b_copy(j, d).wait_send()
        stout(j).wait()
        return 0

    lax.fori_loop(0, NC, drain, 0)
    for c in r2:
        c.wait_recv()
    rg_out[...] = total(zrr)
    for c in r2:
        c.wait_send()


def shards(S, B, tokens, right_factor, left_factor, target):
    rows, cols = tokens.shape
    kl, r, w = right_factor.shape
    cl, lr, nb = left_factor.shape
    Q = S // 2
    NC = 4
    tc = rows // NC
    H = tc // 128
    rrows, lrows = kl * r, (cl // 2) * lr
    folded = left_factor.reshape(cl // 2, 2, lr, nb).transpose(0, 2, 1, 3).reshape(lrows, 2 * nb)
    factors = jnp.concatenate([right_factor.reshape(rrows, w), folded], axis=0)
    cfg = (S, B, NC, tc, kl, cl, nb, w, r, lr)
    V = pltpu.VMEM
    D = pltpu.SemaphoreType.DMA
    student, right, left = pl.pallas_call(
        functools.partial(kernel, cfg),
        out_shape=(
            jax.ShapeDtypeStruct((rows, cols), BF16),
            jax.ShapeDtypeStruct((rrows, w), F32),
            jax.ShapeDtypeStruct((lrows, 2 * nb), F32),
        ),
        in_specs=[pl.BlockSpec(memory_space=pl.ANY)] * 3,
        out_specs=(
            pl.BlockSpec(memory_space=pl.ANY),
            pl.BlockSpec(memory_space=V),
            pl.BlockSpec(memory_space=V),
        ),
        scratch_shapes=[
            V((NC, tc, cols), BF16), V((NC, tc, cols), BF16), V((NC, tc, cols), BF16),
            V((NC, w, kl, tc), BF16), V((NC, B, cl, kl, tc), BF16),
            V((NC, nb, cl, tc), BF16), V((NC, B, kl, cl, tc), BF16),
            V((H, kl * w, 128), F32), V((H, cl * nb, 128), F32),
            V((S, rrows + lrows, w), BF16), V((S, kl, r, w), F32), V((kl, w, w), BF16),
            V((nb, 128), F32), V((cl // 2, 128, 128), BF16), V((cl // 2, 128, 128), BF16),
            V((kl, w, w), F32), V((cl // 2 * nb, 128), F32), V((lrows, 128), F32), V((tc, tc), BF16),
            V((2, Q, rrows, w), BF16), V((Q, rrows, w), BF16), V((Q, rrows, w), BF16), V((Q, rrows, w), BF16),
            V((2, Q, lrows, w), BF16), V((Q, lrows, w), BF16), V((Q, lrows, w), BF16), V((Q, lrows, w), BF16),
            D((2, NC)), D((NC,)), D, D((Q - 1,)), D((Q - 1,)), D((Q,)), D((Q,)),
            D((NC, B - 1)), D((NC, B - 1)), D((NC,)), D((NC, B - 1)), D((NC, B - 1)), D((NC,)),
            D, D, D((Q - 1,)), D((Q - 1,)), D, D, D((Q - 1,)), D((Q - 1,)),
        ],
        compiler_params=pltpu.CompilerParams(
            collective_id=0, has_side_effects=True, vmem_limit_bytes=56 * 1024 * 1024),
        cost_estimate=pl.CostEstimate(
            flops=4 * 1024 * 1024 * 1024, bytes_accessed=3 * rows * cols * 2, transcendentals=rows * cols),
    )(tokens, factors, target)
    left = left.reshape(cl // 2, lr, 2, nb).transpose(0, 2, 1, 3).reshape(cl, lr, nb)
    return student, right.reshape(kl, r, w), left


def solution(mesh):
    return jax.shard_map(
        functools.partial(shards, mesh.shape["seq"], mesh.shape["blk"]),
        mesh=mesh,
        in_specs=(P("seq", "blk"), P("blk", "seq", None), P("blk", "seq", None), P("seq", "blk")),
        out_specs=(P("seq", "blk"), P("blk", "seq", None), P("blk", "seq", None)),
        check_vma=False,
    )
```

time: 233 us -> 135 us (0.58)
  Pallas kernels: 0 us -> 124 us
  waiting for transfers between devices: 122 us -> 0 us
  blocking collectives: 30.5 us -> 0 us
  local copies, waits for them, and re-layouts: 32.3 us -> 8.1 us
  matrix products: 21 us -> 0 us
  between operations: 14.1 us -> 0.65 us
  starting transfers between devices: 9.98 us -> 0 us
    pallas_call x0 -> x1, Pallas kernels: none -> 124 us  [shards(): pl.pallas_call(functools.partial(kernel, cfg), out_shape=(jax.ShapeDtypeS...]
    all_to_all x2 -> x0, waiting for transfers between devices: 69.1 us -> none  [the longest x1 41.6 us: shards(): lax.all_to_all(turned_grad, 'blk', split_axis=1, concat_axis=2, tiled=True)]
    psum x1 -> x0, waiting for transfers between devices: 52.7 us -> none  [shards(): lax.psum(right_term.astype(jnp.bfloat16), 'seq').astype(jnp.float32)]
    all_gather x2 -> x0, blocking collectives: 30.5 us -> none  [the longest x1 16.8 us: shards(): lax.all_gather(right_factor, 'seq', axis=1, tiled=True)]
    dot_general x5 -> x0, matrix products: 21 us -> none  [the longest x1 8.46 us: shards(): jnp.einsum('tkc,cmk->tcm', turned, left_full, preferred_element_type=jnp....]
    convert_element_type x3 -> x0, local copies, waits for them, and re-layouts: 15.6 us -> none  [the longest x1 6.96 us: shards(): target.reshape(rows, local_cols, nblocks).astype(jnp.float32)]
    all_to_all x2 -> x0, starting transfers between devices: 9.76 us -> none  [the longest x1 4.93 us: shards(): lax.all_to_all(mixed, 'blk', split_axis=2, concat_axis=1, tiled=True)]
    all_to_all x2 -> x0, local copies, waits for them, and re-layouts: 5.6 us -> none  [the longest x1 2.8 us: shards(): lax.all_to_all(mixed, 'blk', split_axis=2, concat_axis=1, tiled=True)]
  transfers between devices with their start and end apart: 3 -> 0, of which waited for: 3 -> 0; matrix products, arithmetic and copies ran while one was open for 8% -> 0% of each run, Pallas kernels for 0% -> 0%
where the time goes in v1:
time: 135 us; the launch traced here: 134 us
  Pallas kernels  124 us (92%)
  local copies, waits for them, and re-layouts  8.1 us (6%)
  other arithmetic  1.49 us (1%)
    pallas_call x1, Pallas kernels, shards(): pl.pallas_call(functools.partial(kernel, cfg), out_shape=(jax.ShapeDtypeS...  124 us
    unnamed x4, local copies, waits for them, and re-layouts  5.48 us

profile of v1, /device:TPU:0, one launch (start us, length us, event | category | flops | bytes accessed | tf_op | source)
XLA Modules:
  0.0 134.3 jit_solution(16248822621843594828)
XLA Ops:
  0.6 0.9 copy.10
  1.5 0.1 reshape.26
  1.6 1.5 %pad_maximum_fusion.f_hbm = bf16[384,128]{1,0:T(8,128)(2,1)} fusion(bf16[128,128]{1,0:T(8,128)(2,1)S(1)} %reshape.26, bf16[256,128]{1,0:T(8,128)(2,1)} %bitcast.12), kind=kLoop, calls=%fused_computation | loop fusion | flops 196608 | bytes 196608 | tf_op jit(solution)/shard_map/concatenate | solution.py:311
  3.1 124.1 %shard_map.67 = (bf16[1024,2048]{1,0:T(8,128)(2,1)}, f32[256,128]{1,0:T(8,128)}, f32[128,128]{1,0:T(8,128)}) custom-call(bf16[1024,2048]{1,0:T(8,128)(2,1)} %x_hbm.1, bf16[384,128]{1,0:T(8,128)(2,1)} %pad_maximum_fusion.f_hbm, bf16[1024,2048]{1,0:T(8,128)(2,1)} %t_hbm.1), custom_call_target="tpu_custom_call" | custom-call | flops 4294967296 | bytes 12582912 | tf_op jit(solution)/shard_map/pallas_call | solution.py:315
  127.2 1.0 reshape.28
  128.2 0.7 copy.8
  128.9 0.0 copy-start
  128.9 4.8 %copy.13 = bf16[1024,2048]{1,0:T(8,128)(2,1)} copy(bf16[1024,2048]{1,0:T(8,128)(2,1)} %get-tuple-element.12) | data formatting | bytes 8388608
  133.7 0.0 copy-done
  133.7 0.7 copy.14
Async XLA Ops:
  128.9 4.8 %copy-start = (f32[256,128]{1,0:T(8,128)S(1)}, f32[256,128]{1,0:T(8,128)}, u32[]{:S(2)}) copy-start(f32[256,128]{1,0:T(8,128)} %get-tuple-element.7) | copy-start | bytes 393220

commit v2 on v1

--- a/solution.py
+++ b/solution.py
@@ -42,11 +42,11 @@
 
 
 def kernel(
-    cfg, x_hbm, f_hbm, t_hbm, st_hbm, rg_out, lg_out,
+    cfg, x_hbm, r_hbm, l_ref, t_hbm, st_hbm, rg_out, lg_out,
     xv, tv, stv, snd, recv, bsnd, brecv, fm, ft,
-    gat, gf, rfull, lc, wb, wt, rg, lg, lga, idt,
+    gat, gatl, lfold, gf, rfull, lc, wb, wt, rg, lg, lga, idt,
     pbr, sibr, zsr, zrr, pbl, sibl, zsl, zrl,
-    sx, sto, sf, gs, gr, fs, fr,
+    sx, sto, sf, gs, gr, fs, fr, hs, hr, is_, ir,
     as_, ar, al, bs, br, bl,
     rs1, rr1, rs2, rr2, ls1, lr1, ls2, lr2,
 ):
@@ -72,45 +72,60 @@
     def stout(j):
         return pltpu.make_async_copy(stv.at[j], st_hbm.at[pl.ds(pl.multiple_of(j * tc, tc), tc)], sto.at[j])
 
-    own = pltpu.make_async_copy(f_hbm, gat.at[s], sf)
+    own = pltpu.make_async_copy(r_hbm, gat.at[s], sf)
     own.start()
     for j in range(NC):
         xload(j).start()
-    for j in range(NC):
-        tload(j).start()
 
     barrier = pltpu.get_barrier_semaphore()
     for peer in [sib] + zpeers + bpeers:
         pl.semaphore_signal(barrier, inc=1, device_id=peer, device_id_type=MESH)
     pl.semaphore_wait(barrier, 1 + len(zpeers) + len(bpeers))
 
-    own.wait()
-    gsend = [
-        pltpu.make_async_remote_copy(
-            gat.at[s], gat.at[s], gs.at[o], gr.at[o], device_id=zpeers[o], device_id_type=MESH)
-        for o in range(Q - 1)
-    ]
+    def spread(first, buf, ss, rs):
+        return [
+            pltpu.make_async_remote_copy(
+                first, buf.at[s], ss.at[o], rs.at[o], device_id=zpeers[o], device_id_type=MESH)
+            for o in range(Q - 1)
+        ]
+
+    def pass_on(first, buf, ss, rs):
+        out = []
+        for o in range(Q):
+            src = ((q - o + Q) % Q) * 2 + core
+            out.append(pltpu.make_async_remote_copy(
+                buf.at[src] if o else first, buf.at[src], ss.at[o], rs.at[o],
+                device_id=sib, device_id_type=MESH))
+        return out
+
+    gsend = spread(r_hbm, gat, gs, gr)
+    fsend = pass_on(r_hbm, gat, fs, fr)
     for c in gsend:
         c.start()
-
-    def fwd_copy(o):
-        src = ((q - o + Q) % Q) * 2 + core
-        return pltpu.make_async_remote_copy(
-            gat.at[src], gat.at[src], fs.at[o], fr.at[o], device_id=sib, device_id_type=MESH)
-
-    fsend = [fwd_copy(o) for o in range(Q)]
     fsend[0].start()
+    for j in range(NC):
+        tload(j).start()
     idt[...] = eye(tc)
     rg[...] = jnp.zeros_like(rg)
     lg[...] = jnp.zeros_like(lg)
+    for p in range(cl // 2):
+        lfold[p * lr:(p + 1) * lr, :] = jnp.concatenate(
+            [l_ref[2 * p].astype(F32), l_ref[2 * p + 1].astype(F32)], axis=1)
+    gatl[s] = lfold[...].astype(BF16)
+    own.wait()
     for o in range(1, Q):
         gsend[o - 1].wait_recv()
         fsend[o].start()
+    hsend = spread(gatl.at[s], gatl, hs, hr)
+    isend = pass_on(gatl.at[s], gatl, is_, ir)
+    for c in hsend:
+        c.start()
+    isend[0].start()
     for o in range(Q):
         fsend[o].wait_recv()
 
     for i in range(S):
-        gf[i] = gat[i, :rrows, :].astype(F32).reshape(kl, r, w)
+        gf[i] = gat[i].astype(F32).reshape(kl, r, w)
 
     def rbuild(k, _):
         rfull[k] = jnp.concatenate([gf[i, k] for i in range(S)], axis=0).astype(BF16)
@@ -153,11 +168,17 @@
 
     lax.fori_loop(0, NC, forward, 0)
 
+    for o in range(1, Q):
+        hsend[o - 1].wait_recv()
+        isend[o].start()
+    for o in range(Q):
+        isend[o].wait_recv()
+
     gl = fm.at[0]
     lcols = lax.broadcasted_iota(jnp.int32, (nb, 128), 1)
     for i in range(S):
-        gl[i * lrows:(i + 1) * lrows, :] = gat[i, rrows:rrows + lrows, :].astype(F32)
-    e128 = eye(128)
+        gl[i * lrows:(i + 1) * lrows, :] = gatl[i].astype(F32)
+    e128 = idt[:128, :128]
 
     def lbuild(p, _):
         for m in range(lr):
@@ -190,7 +211,7 @@
             tp = stack([recv[j, a, 2 * p + c] for c in range(2) for a in range(B)])
             cols = pl.ds(pl.multiple_of(p * 128, 128), 128)
             v = dot(wb[p], tp, NN)
-            tgt = dot(idt[:128, :128], tv[j, :, cols], NT)
+            tgt = dot(e128, tv[j, :, cols], NT)
             v2 = v * v
             th = jnp.tanh(v * (C0 + (C0 * 0.044715) * v2))
             half = 0.5 + 0.5 * th
@@ -280,7 +301,7 @@
     lg_out[...] = total(zrl)
     r1.wait_recv()
     r2 = second(pbr, sibr, zsr, zrr, rs2, rr2)
-    for c in gsend + fsend + [l1, r1] + l2:
+    for c in gsend + fsend + hsend + isend + [l1, r1] + l2:
         c.wait_send()
 
     def drain(j, _):
@@ -298,17 +319,28 @@
         c.wait_send()
 
 
+def finish(st_ref, rg_ref, lg_ref, st_out, rg_out, lg_out):
+    st_out[...] = st_ref[...]
+
+    @pl.when(pl.program_id(0) == 0)
+    def _():
+        rg_out[...] = rg_ref[...].reshape(rg_out.shape)
+        cl, lr, nb = lg_out.shape
+        for p in range(cl // 2):
+            v = lg_ref[p * lr:(p + 1) * lr, :]
+            lg_out[2 * p] = v[:, :nb]
+            lg_out[2 * p + 1] = v[:, nb:]
+
+
 def shards(S, B, tokens, right_factor, left_factor, target):
     rows, cols = tokens.shape
     kl, r, w = right_factor.shape
     cl, lr, nb = left_factor.shape
     Q = S // 2
-    NC = 4
+    NC = 8
     tc = rows // NC
     H = tc // 128
     rrows, lrows = kl * r, (cl // 2) * lr
-    folded = left_factor.reshape(cl // 2, 2, lr, nb).transpose(0, 2, 1, 3).reshape(lrows, 2 * nb)
-    factors = jnp.concatenate([right_factor.reshape(rrows, w), folded], axis=0)
     cfg = (S, B, NC, tc, kl, cl, nb, w, r, lr)
     V = pltpu.VMEM
     D = pltpu.SemaphoreType.DMA
@@ -319,7 +351,12 @@
             jax.ShapeDtypeStruct((rrows, w), F32),
             jax.ShapeDtypeStruct((lrows, 2 * nb), F32),
         ),
-        in_specs=[pl.BlockSpec(memory_space=pl.ANY)] * 3,
+        in_specs=[
+            pl.BlockSpec(memory_space=pl.ANY),
+            pl.BlockSpec(memory_space=pl.ANY),
+            pl.BlockSpec(memory_space=V),
+            pl.BlockSpec(memory_space=pl.ANY),
+        ],
         out_specs=(
             pl.BlockSpec(memory_space=pl.ANY),
             pl.BlockSpec(memory_space=V),
@@ -330,12 +367,12 @@
             V((NC, w, kl, tc), BF16), V((NC, B, cl, kl, tc), BF16),
             V((NC, nb, cl, tc), BF16), V((NC, B, kl, cl, tc), BF16),
             V((H, kl * w, 128), F32), V((H, cl * nb, 128), F32),
-            V((S, rrows + lrows, w), BF16), V((S, kl, r, w), F32), V((kl, w, w), BF16),
+            V((S, rrows, w), BF16), V((S, lrows, w), BF16), V((lrows, w), F32), V((S, kl, r, w), F32), V((kl, w, w), BF16),
             V((nb, 128), F32), V((cl // 2, 128, 128), BF16), V((cl // 2, 128, 128), BF16),
             V((kl, w, w), F32), V((cl // 2 * nb, 128), F32), V((lrows, 128), F32), V((tc, tc), BF16),
             V((2, Q, rrows, w), BF16), V((Q, rrows, w), BF16), V((Q, rrows, w), BF16), V((Q, rrows, w), BF16),
             V((2, Q, lrows, w), BF16), V((Q, lrows, w), BF16), V((Q, lrows, w), BF16), V((Q, lrows, w), BF16),
-            D((2, NC)), D((NC,)), D, D((Q - 1,)), D((Q - 1,)), D((Q,)), D((Q,)),
+            D((2, NC)), D((NC,)), D, D((Q - 1,)), D((Q - 1,)), D((Q,)), D((Q,)), D((Q - 1,)), D((Q - 1,)), D((Q,)), D((Q,)),
             D((NC, B - 1)), D((NC, B - 1)), D((NC,)), D((NC, B - 1)), D((NC, B - 1)), D((NC,)),
             D, D, D((Q - 1,)), D((Q - 1,)), D, D, D((Q - 1,)), D((Q - 1,)),
         ],
@@ -343,9 +380,29 @@
             collective_id=0, has_side_effects=True, vmem_limit_bytes=56 * 1024 * 1024),
         cost_estimate=pl.CostEstimate(
             flops=4 * 1024 * 1024 * 1024, bytes_accessed=3 * rows * cols * 2, transcendentals=rows * cols),
-    )(tokens, factors, target)
-    left = left.reshape(cl // 2, lr, 2, nb).transpose(0, 2, 1, 3).reshape(cl, lr, nb)
-    return student, right.reshape(kl, r, w), left
+    )(tokens, right_factor.reshape(rrows, w), left_factor, target)
+    steps = 4
+    return pl.pallas_call(
+        finish,
+        grid=(steps,),
+        out_shape=(
+            jax.ShapeDtypeStruct((rows, cols), BF16),
+            jax.ShapeDtypeStruct((kl, r, w), F32),
+            jax.ShapeDtypeStruct((cl, lr, nb), F32),
+        ),
+        in_specs=[
+            pl.BlockSpec((rows // steps, cols), lambda i: (i, 0)),
+            pl.BlockSpec((rrows, w), lambda i: (0, 0)),
+            pl.BlockSpec((lrows, 2 * nb), lambda i: (0, 0)),
+        ],
+        out_specs=(
+            pl.BlockSpec((rows // steps, cols), lambda i: (i, 0)),
+            pl.BlockSpec((kl, r, w), lambda i: (0, 0, 0)),
+            pl.BlockSpec((cl, lr, nb), lambda i: (0, 0, 0)),
+        ),
+        compiler_params=pltpu.CompilerParams(vmem_limit_bytes=60 * 1024 * 1024),
+        cost_estimate=pl.CostEstimate(flops=0, bytes_accessed=4 * rows * cols, transcendentals=0),
+    )(student, right, left)
 
 
 def solution(mesh):

time: 135 us -> 134 us (level)
  Pallas kernels: 124 us -> 133 us
  local copies, waits for them, and re-layouts: 8.1 us -> 0 us
  other arithmetic: 1.49 us -> 0 us
    unnamed x4 -> x0, local copies, waits for them, and re-layouts: 5.48 us -> none
    pallas_call x0 -> x1, Pallas kernels: none -> 4.89 us  [shards(): pl.pallas_call(finish, grid=(steps,), out_shape=(jax.ShapeDtypeStruct((ro...]
    pallas_call x1, Pallas kernels: 124 us -> 128 us  [shards(): pl.pallas_call(functools.partial(kernel, cfg), out_shape=(jax.ShapeDtypeS...]
    reshape x3 -> x0, local copies, waits for them, and re-layouts: 1.95 us -> none  [the longest x2 0.99 us: shards(): left_factor.reshape(cl // 2, 2, lr, nb).transpose(0, 2, 1, 3)]
    concatenate x1 -> x0, other arithmetic: 1.49 us -> none  [shards(): factors = jnp.concatenate([right_factor.reshape(rrows, w), folded], axis=0)]
where the time goes in v2:
time: 134 us; the launch traced here: 133 us
  Pallas kernels  133 us (99%)
    pallas_call x1, Pallas kernels, shards(): pl.pallas_call(functools.partial(kernel, cfg), out_shape=(jax.ShapeDtypeS...  128 us
    pallas_call x1, Pallas kernels, shards(): pl.pallas_call(finish, grid=(steps,), out_shape=(jax.ShapeDtypeStruct((ro...  4.89 us

profile of v2, /device:TPU:0, one launch (start us, length us, event | category | flops | bytes accessed | tf_op | source)
XLA Modules:
  0.0 133.4 jit_solution(11422550960983745330)
XLA Ops:
  0.6 127.9 %shard_map.67 = (bf16[1024,2048]{1,0:T(8,128)(2,1)}, f32[256,128]{1,0:T(8,128)}, f32[128,128]{1,0:T(8,128)}) custom-call(bf16[1024,2048]{1,0:T(8,128)(2,1)} %x_hbm.1, bf16[256,128]{1,0:T(8,128)(2,1)} %bitcast.1, bf16[32,8,64]{2,1,0:T(8,128)(2,1)} %l_ref.1, bf16[1024,2048]{1,0:T(8,128)(2,1)} %t_hbm.1), custom_call_target="tpu_custom_call" | custom-call | flops 4294967296 | bytes 12582912 | tf_op jit(solution)/shard_map/pallas_call | solution.py:347
  128.5 4.9 %shard_map.68 = (bf16[1024,2048]{1,0:T(8,128)(2,1)}, f32[16,16,128]{2,1,0:T(8,128)}, f32[32,8,64]{2,1,0:T(8,128)}) custom-call(bf16[1024,2048]{1,0:T(8,128)(2,1)} %get-tuple-element.6.st_ref, f32[256,128]{1,0:T(8,128)} %get-tuple-element.7.rg_ref, f32[128,128]{1,0:T(8,128)} %get-tuple-element.8.lg_ref), custom_call_target="tpu_custom_call" | custom-call | bytes 8388608 | tf_op jit(solution)/shard_map/pallas_call | solution.py:385

commit v3 on v2

--- a/solution.py
+++ b/solution.py
@@ -145,13 +145,15 @@
     def forward(j, _):
         xload(j).wait()
 
-        def mm(k, _):
-            res = dot(rfull[k], xv[j, :, pl.ds(pl.multiple_of(k * w, w), w)], NT)
-            for h in range(H):
-                fm[h, pl.ds(pl.multiple_of(k * w, w), w), :] = res[:, h * 128:(h + 1) * 128]
+        def mm(g, _):
+            ks = [g * 4 + u for u in range(4)]
+            res = [dot(rfull[k], xv[j, :, pl.ds(pl.multiple_of(k * w, w), w)], NT) for k in ks]
+            for k, v in zip(ks, res):
+                for h in range(H):
+                    fm[h, pl.ds(pl.multiple_of(k * w, w), w), :] = v[:, h * 128:(h + 1) * 128]
             return 0
 
-        lax.fori_loop(0, kl, mm, 0)
+        lax.fori_loop(0, kl // 4, mm, 0)
 
         def turn(g, _):
             for u in range(8):
@@ -207,27 +209,35 @@
         for d in range(B - 1):
             a_copy(j, d).wait_recv()
 
-        def pair(p, _):
-            tp = stack([recv[j, a, 2 * p + c] for c in range(2) for a in range(B)])
-            cols = pl.ds(pl.multiple_of(p * 128, 128), 128)
-            v = dot(wb[p], tp, NN)
-            tgt = dot(e128, tv[j, :, cols], NT)
-            v2 = v * v
-            th = jnp.tanh(v * (C0 + (C0 * 0.044715) * v2))
-            half = 0.5 + 0.5 * th
-            act = v * half
-            deriv = half + 0.5 * v * (1.0 - th * th) * (C0 + (3.0 * 0.044715 * C0) * v2)
-            pg = (((act - tgt) * scale) * deriv).astype(BF16)
-            stv[j, :, cols] = dot(idt[...], act.astype(BF16), NT).astype(BF16)
-            tg = dot(wt[p], pg, NN)
-            for h in range(H):
-                ft[h, pl.ds(pl.multiple_of(p * 128, 128), 128), :] = tg[:, h * 128:(h + 1) * 128]
-            full = dot(pg, tp, NT)
-            rows = pl.ds(pl.multiple_of(p * nb, nb), nb)
-            lg[rows, :] += jnp.where(lcols < nb, full[:nb], full[nb:])
+        def pairs(g, _):
+            ps = [g * 4 + u for u in range(4)]
+            cols = [pl.ds(pl.multiple_of(p * 128, 128), 128) for p in ps]
+            tps = [stack([recv[j, a, 2 * p + c] for c in range(2) for a in range(B)]) for p in ps]
+            vs = [dot(wb[p], tp, NN) for p, tp in zip(ps, tps)]
+            tgts = [dot(e128, tv[j, :, c], NT) for c in cols]
+            acts, pgs = [], []
+            for v, tgt in zip(vs, tgts):
+                v2 = v * v
+                th = jnp.tanh(v * (C0 + (C0 * 0.044715) * v2))
+                half = 0.5 + 0.5 * th
+                act = v * half
+                deriv = half + 0.5 * v * (1.0 - th * th) * (C0 + (3.0 * 0.044715 * C0) * v2)
+                acts.append(act.astype(BF16))
+                pgs.append((((act - tgt) * scale) * deriv).astype(BF16))
+            tgs = [dot(wt[p], pg, NN) for p, pg in zip(ps, pgs)]
+            sts = [dot(idt[...], act, NT).astype(BF16) for act in acts]
+            fulls = [dot(pg, tp, NT) for pg, tp in zip(pgs, tps)]
+            for p, tg in zip(ps, tgs):
+                for h in range(H):
+                    ft[h, pl.ds(pl.multiple_of(p * 128, 128), 128), :] = tg[:, h * 128:(h + 1) * 128]
+            for c, st in zip(cols, sts):
+                stv[j, :, c] = st
+            for p, full in zip(ps, fulls):
+                rows = pl.ds(pl.multiple_of(p * nb, nb), nb)
+                lg[rows, :] += jnp.where(lcols < nb, full[:nb], full[nb:])
             return 0
 
-        lax.fori_loop(0, cl // 2, pair, 0)
+        lax.fori_loop(0, cl // 8, pairs, 0)
 
         def turn(g, _):
             for u in range(4):
@@ -258,12 +268,15 @@
         for d in range(B - 1):
             b_copy(j, d).wait_recv()
 
-        def one(k, _):
-            mg = stack([brecv[j, a, k] for a in range(B)])
-            rg[k] += dot(mg, xv[j, :, pl.ds(pl.multiple_of(k * w, w), w)], NN)
+        def blocks(g, _):
+            ks = [g * 4 + u for u in range(4)]
+            mgs = [stack([brecv[j, a, k] for a in range(B)]) for k in ks]
+            res = [dot(mg, xv[j, :, pl.ds(pl.multiple_of(k * w, w), w)], NN) for k, mg in zip(ks, mgs)]
+            for k, v in zip(ks, res):
+                rg[k] += v
             return 0
 
-        lax.fori_loop(0, kl, one, 0)
+        lax.fori_loop(0, kl // 4, blocks, 0)
         return 0
 
     def second(pb, sibv, zs, zr, ss, rs):
@@ -337,7 +350,7 @@
     kl, r, w = right_factor.shape
     cl, lr, nb = left_factor.shape
     Q = S // 2
-    NC = 8
+    NC = 4
     tc = rows // NC
     H = tc // 128
     rrows, lrows = kl * r, (cl // 2) * lr
@@ -381,7 +394,7 @@
         cost_estimate=pl.CostEstimate(
             flops=4 * 1024 * 1024 * 1024, bytes_accessed=3 * rows * cols * 2, transcendentals=rows * cols),
     )(tokens, right_factor.reshape(rrows, w), left_factor, target)
-    steps = 4
+    steps = 8
     return pl.pallas_call(
         finish,
         grid=(steps,),

time: 134 us -> 125 us (0.933)
  Pallas kernels: 133 us -> 124 us
    pallas_call x1, Pallas kernels: 128 us -> 118 us  [shards(): pl.pallas_call(functools.partial(kernel, cfg), out_shape=(jax.ShapeDtypeS...]
    pallas_call x1, Pallas kernels: 4.89 us -> 6.75 us  [shards(): pl.pallas_call(finish, grid=(steps,), out_shape=(jax.ShapeDtypeStruct((ro...]
where the time goes in v3:
time: 125 us
  Pallas kernels  124 us (99%)
    pallas_call x1, Pallas kernels, shards(): pl.pallas_call(functools.partial(kernel, cfg), out_shape=(jax.ShapeDtypeS...  118 us
    pallas_call x1, Pallas kernels, shards(): pl.pallas_call(finish, grid=(steps,), out_shape=(jax.ShapeDtypeStruct((ro...  6.75 us

profile of v3, /device:TPU:0, one launch (start us, length us, event | category | flops | bytes accessed | tf_op | source)
XLA Modules:
  0.0 125.1 jit_solution(2429003488194039496)
XLA Ops:
  0.6 117.7 %shard_map.67 = (bf16[1024,2048]{1,0:T(8,128)(2,1)}, f32[256,128]{1,0:T(8,128)}, f32[128,128]{1,0:T(8,128)}) custom-call(bf16[1024,2048]{1,0:T(8,128)(2,1)} %x_hbm.1, bf16[256,128]{1,0:T(8,128)(2,1)} %bitcast.1, bf16[32,8,64]{2,1,0:T(8,128)(2,1)} %l_ref.1, bf16[1024,2048]{1,0:T(8,128)(2,1)} %t_hbm.1), custom_call_target="tpu_custom_call" | custom-call | flops 4294967296 | bytes 12582912 | tf_op jit(solution)/shard_map/pallas_call | solution.py:360
  118.3 6.7 %shard_map.68 = (bf16[1024,2048]{1,0:T(8,128)(2,1)}, f32[16,16,128]{2,1,0:T(8,128)}, f32[32,8,64]{2,1,0:T(8,128)}) custom-call(bf16[1024,2048]{1,0:T(8,128)(2,1)} %get-tuple-element.6.st_ref, f32[256,128]{1,0:T(8,128)} %get-tuple-element.7.rg_ref, f32[128,128]{1,0:T(8,128)} %get-tuple-element.8.lg_ref), custom_call_target="tpu_custom_call" | custom-call | bytes 8388608 | tf_op jit(solution)/shard_map/pallas_call | solution.py:398

commit v4 on v3

--- a/solution.py
+++ b/solution.py
@@ -163,12 +163,16 @@
             return 0
 
         lax.fori_loop(0, w // 8, turn, 0)
+        a_local(j).start()
+        return 0
+
+    def launch(j, _):
+        forward(j, 0)
         for d in range(B - 1):
             a_copy(j, d).start()
-        a_local(j).start()
-        return 0
-
-    lax.fori_loop(0, NC, forward, 0)
+        return 0
+
+    lax.fori_loop(0, 2, launch, 0)
 
     for o in range(1, Q):
         hsend[o - 1].wait_recv()
@@ -186,10 +190,10 @@
         for m in range(lr):
             lc[pl.ds(m, S, stride=lr), :] = gl[pl.ds(p * lr + m, S, stride=lrows), :]
         v = lc[...]
-        both = jnp.concatenate(
+        block = jnp.concatenate(
             [jnp.where(lcols < nb, v, 0.0), jnp.where(lcols >= nb, v, 0.0)], axis=0).astype(BF16)
-        wb[p] = both
-        wt[p] = dot(e128, both, NT).astype(BF16)
+        wb[p] = block
+        wt[p] = dot(e128, block, NT).astype(BF16)
         return 0
 
     lax.fori_loop(0, cl // 2, lbuild, 0)
@@ -253,7 +257,15 @@
         stout(j).start()
         return 0
 
-    lax.fori_loop(0, NC, middle, 0)
+    def both(j, _):
+        forward(j + 2, 0)
+        for d in range(B - 1):
+            a_copy(j, d).wait_send()
+            a_copy(j + 2, d).start()
+        return middle(j, 0)
+
+    lax.fori_loop(0, NC - 2, both, 0)
+    lax.fori_loop(NC - 2, NC, middle, 0)
 
     l1 = pltpu.make_async_remote_copy(
         pbl.at[1 - core], sibl, ls1, lr1, device_id=sib, device_id_type=MESH)
@@ -319,12 +331,14 @@
 
     def drain(j, _):
         for d in range(B - 1):
-            a_copy(j, d).wait_send()
             b_copy(j, d).wait_send()
         stout(j).wait()
         return 0
 
     lax.fori_loop(0, NC, drain, 0)
+    for j in (NC - 2, NC - 1):
+        for d in range(B - 1):
+            a_copy(j, d).wait_send()
     for c in r2:
         c.wait_recv()
     rg_out[...] = total(zrr)
@@ -394,7 +408,7 @@
         cost_estimate=pl.CostEstimate(
             flops=4 * 1024 * 1024 * 1024, bytes_accessed=3 * rows * cols * 2, transcendentals=rows * cols),
     )(tokens, right_factor.reshape(rrows, w), left_factor, target)
-    steps = 8
+    steps = 4
     return pl.pallas_call(
         finish,
         grid=(steps,),

time: 125 us -> 124 us (level)
    pallas_call x1, Pallas kernels: 6.75 us -> 4.89 us  [shards(): pl.pallas_call(finish, grid=(steps,), out_shape=(jax.ShapeDtypeStruct((ro...]
where the time goes in v4:
time: 124 us; the launch traced here: 123 us
  Pallas kernels  123 us (99%)
    pallas_call x1, Pallas kernels, shards(): pl.pallas_call(functools.partial(kernel, cfg), out_shape=(jax.ShapeDtypeS...  118 us
    pallas_call x1, Pallas kernels, shards(): pl.pallas_call(finish, grid=(steps,), out_shape=(jax.ShapeDtypeStruct((ro...  4.89 us

profile of v4, /device:TPU:0, one launch (start us, length us, event | category | flops | bytes accessed | tf_op | source)
XLA Modules:
  0.0 123.3 jit_solution(13599627979352153894)
XLA Ops:
  0.6 117.7 %shard_map.67 = (bf16[1024,2048]{1,0:T(8,128)(2,1)}, f32[256,128]{1,0:T(8,128)}, f32[128,128]{1,0:T(8,128)}) custom-call(bf16[1024,2048]{1,0:T(8,128)(2,1)} %x_hbm.1, bf16[256,128]{1,0:T(8,128)(2,1)} %bitcast.1, bf16[32,8,64]{2,1,0:T(8,128)(2,1)} %l_ref.1, bf16[1024,2048]{1,0:T(8,128)(2,1)} %t_hbm.1), custom_call_target="tpu_custom_call" | custom-call | flops 4294967296 | bytes 12582912 | tf_op jit(solution)/shard_map/pallas_call | solution.py:374
  118.4 4.9 %shard_map.68 = (bf16[1024,2048]{1,0:T(8,128)(2,1)}, f32[16,16,128]{2,1,0:T(8,128)}, f32[32,8,64]{2,1,0:T(8,128)}) custom-call(bf16[1024,2048]{1,0:T(8,128)(2,1)} %get-tuple-element.6.st_ref, f32[256,128]{1,0:T(8,128)} %get-tuple-element.7.rg_ref, f32[128,128]{1,0:T(8,128)} %get-tuple-element.8.lg_ref), custom_call_target="tpu_custom_call" | custom-call | bytes 8388608 | tf_op jit(solution)/shard_map/pallas_call | solution.py:412
